TPU v7x, 32 devices: a whole 2x2x4 slice. The times are simulated.
32 devices in a mesh: groups: 2 (over y), gene: 8 (over z, x), cell: 2 (over core).
Axes of the slice: x: 2, y: 2, z: 4, core: 2. Of those that a mesh axis runs over, the one named last changes fastest.
Arguments:
- control: bfloat16 [512, 32768], P(('groups', 'cell'), 'gene'), parts along dimension 0, may hold values from -6 to 6
- perturbed: bfloat16 [512, 32768], P(('groups', 'cell'), 'gene'), parts along dimension 0, may hold values from -6 to 6
- pair_index: int32 [4, 128], P(('groups', 'cell')), parts along dimension 0, may hold values from 0 to 127, each once within a row
- noise_draws: bfloat16 [512, 2, 128], P(('groups', 'cell')), parts along dimension 0, may hold values from -6 to 6
- cell_mass: float32 [512], P(('groups', 'cell')), parts along dimension 0, may hold values from 0.25 to 4
- w_enc: bfloat16 [32768, 4096], P(('gene', 'cell')), may hold values from -0.03125 to 0.03125
- w_dec: bfloat16 [32768, 4096], P(('gene', 'cell')), may hold values from -0.09375 to 0.09375
- w_crit: bfloat16 [32768, 4096], P(('gene', 'cell')), may hold values from -0.03125 to 0.03125
- w_noise: bfloat16 [128, 4096], P(None, 'gene'), may hold values from -0.5 to 0.5
- readout: float32 [4096], P('gene'), may hold values from -0.09375 to 0.09375
Outputs:
- grad_enc: bfloat16 [65536, 4096], P(('groups', 'gene', 'cell')), parts along dimension 0
- grad_dec: bfloat16 [65536, 4096], P(('groups', 'gene', 'cell')), parts along dimension 0
There are 2 independent parts, one for each index of `groups`. A program takes and returns all parts, laid end to end along the dimension named above; an argument that names none is the same for every part. Nothing has to cross between parts.
Inputs may be any that keep to these rules, and one draw needn't show every extreme that they name: Each row of pair_index is a permutation of 0 to 127.
All inputs are finite; a program needn't handle non-finite values.
Results may differ from a plain program's by a relative error of at most 0.0065.
Values may be sent and summed in bfloat16 or wider, within the bound.
A program may use at most 512 MiB of HBM per device.

v0:
```python
import math

import jax
import jax.numpy as jnp
from jax import lax
from jax.sharding import PartitionSpec as P

G = 32768


def silu_grad(inputs):
    sigmoid = jax.nn.sigmoid(inputs)
    return sigmoid * (1.0 + inputs * (1.0 - sigmoid))


def contract(former, latter, former_dim, latter_dim):
    return lax.dot_general(
        former,
        latter,
        (((former_dim,), (latter_dim,)), ((), ())),
        preferred_element_type=jnp.float32,
    )


def paired_rows(perturbed, pair_index):
    n_rows = perturbed.shape[0]
    per_block = pair_index.shape[1]
    offsets = (jnp.arange(pair_index.shape[0], dtype=jnp.int32) * per_block)[:, None]
    chosen = (pair_index + offsets).reshape(n_rows)
    one_hot = (chosen[:, None] == jnp.arange(n_rows, dtype=jnp.int32)[None, :]).astype(
        perturbed.dtype
    )
    return jnp.dot(one_hot, perturbed, preferred_element_type=jnp.float32).astype(perturbed.dtype)


def train_step(
    control,
    target,
    noise_draws,
    cell_mass,
    w_enc,
    w_dec,
    w_crit,
    noise_cols,
    readout_cols,
    transfers,
):
    spread_enc, gather_lat, spread_crit, fold_crit, spread_lat, map_enc = transfers
    n_cells, n_genes = control.shape
    n_draws = noise_draws.shape[1]
    n_pairs = n_cells * n_draws
    hidden = w_enc.shape[1]

    def enc_term(offset, extent):
        return contract(w_enc, control, 0, 1)

    enc_share = spread_enc(enc_term, hidden)
    n_share = enc_share.shape[0]
    flat_noise = noise_draws.reshape(n_pairs, noise_draws.shape[2])
    noise_shift = contract(noise_cols, flat_noise, 0, 1).reshape(n_share, n_cells, n_draws)
    latent_share = (
        (jax.nn.silu(enc_share)[:, :, None] + noise_shift)
        .astype(jnp.bfloat16)
        .reshape(n_share, n_pairs)
    )
    latent = gather_lat(latent_share)
    decoded = contract(latent, w_dec, 0, 1).reshape(n_cells, n_draws, n_genes)
    moved_cells = (
        (control.astype(jnp.float32)[:, None, :] + decoded)
        .astype(jnp.bfloat16)
        .reshape(n_pairs, n_genes)
    )

    def crit_term(offset, extent):
        return contract(w_crit, moved_cells, 0, 1)

    critic_pre = spread_crit(crit_term, hidden)
    weight = 8.0 / n_draws * jnp.repeat(cell_mass, n_draws)
    critic_grad = (-weight[None, :] * readout_cols[:, None] * silu_grad(critic_pre)).astype(
        jnp.bfloat16
    )

    def add_back(running, portion, offset):
        extent = portion.shape[0]
        return contract(portion, w_crit, 0, 1)

    critic_back = fold_crit(critic_grad, add_back, jnp.zeros((n_pairs, n_genes), jnp.float32))
    moved_f32 = moved_cells.astype(jnp.float32).reshape(n_cells, n_draws, n_genes)
    mean_moved = jnp.sum(moved_f32, axis=1, keepdims=True) / n_draws
    cost_grad = (
        8.0
        / (n_draws * math.sqrt(G))
        * cell_mass[:, None, None]
        * (0.5 * moved_f32 + 0.5 * mean_moved - target.astype(jnp.float32)[:, None, :])
    )
    moved_grad = (cost_grad.reshape(n_pairs, n_genes) + critic_back).astype(jnp.bfloat16)
    grad_dec = contract(moved_grad, latent, 0, 1)

    def lat_term(offset, extent):
        return contract(w_dec, moved_grad, 0, 1)

    latent_grad = spread_lat(lat_term, hidden)
    enc_grad = (
        silu_grad(enc_share) * jnp.sum(latent_grad.reshape(n_share, n_cells, n_draws), axis=2)
    ).astype(jnp.bfloat16)

    def enc_cols(portion, offset):
        return contract(control, portion, 0, 1)

    grad_enc = map_enc(enc_grad, enc_cols)
    return (grad_enc, grad_dec)


def shards(
    control, perturbed, pair_index, noise_draws, cell_mass, w_enc, w_dec, w_crit, w_noise, readout
):
    target = paired_rows(perturbed, pair_index)

    def spread_enc(producer, n_rows):
        return lax.psum_scatter(
            producer(
                jnp.int32(0),
                n_rows // lax.axis_size(("gene", "cell")) * lax.axis_size(("gene", "cell")),
            ),
            ("gene", "cell"),
            scatter_dimension=0,
            tiled=True,
        )

    def gather_lat(latent_share):
        return lax.all_gather(latent_share, ("gene", "cell"), axis=0, tiled=True)

    def spread_crit(producer, n_rows):
        return lax.psum_scatter(
            producer(
                jnp.int32(0),
                n_rows // lax.axis_size(("gene", "cell")) * lax.axis_size(("gene", "cell")),
            ),
            ("gene", "cell"),
            scatter_dimension=0,
            tiled=True,
        )

    def fold_crit(critic_grad, folder, initial):
        return folder(
            initial, lax.all_gather(critic_grad, ("gene", "cell"), axis=0, tiled=True), jnp.int32(0)
        )

    def spread_lat(producer, n_rows):
        return lax.psum_scatter(
            producer(
                jnp.int32(0),
                n_rows // lax.axis_size(("gene", "cell")) * lax.axis_size(("gene", "cell")),
            ),
            ("gene", "cell"),
            scatter_dimension=0,
            tiled=True,
        )

    def map_enc(enc_grad, mapper):
        return mapper(lax.all_gather(enc_grad, ("gene", "cell"), axis=0, tiled=True), jnp.int32(0))

    control_all, target_all = (
        lax.all_to_all(control, "cell", split_axis=1, concat_axis=0, tiled=True),
        lax.all_to_all(target, "cell", split_axis=1, concat_axis=0, tiled=True),
    )
    noise_all, mass_all = (
        lax.all_gather(noise_draws.astype(jnp.float32), "cell", axis=0, tiled=True),
        lax.all_gather(cell_mass, "cell", axis=0, tiled=True),
    )
    half_width = w_noise.shape[1] // 2
    offset = lax.axis_index("cell") * half_width
    noise_cols = lax.dynamic_slice_in_dim(w_noise, offset, half_width, 1)
    readout_cols = lax.dynamic_slice_in_dim(readout, offset, half_width, 0)
    transfers = (spread_enc, gather_lat, spread_crit, fold_crit, spread_lat, map_enc)
    grad_enc, grad_dec = train_step(
        control_all,
        target_all,
        noise_all.astype(jnp.bfloat16),
        mass_all,
        w_enc,
        w_dec,
        w_crit,
        noise_cols,
        readout_cols,
        transfers,
    )
    return (grad_enc.astype(jnp.bfloat16), grad_dec.astype(jnp.bfloat16))


def solution(mesh):
    placed = (
        P(("groups", "cell"), "gene"),
        P(("groups", "cell"), "gene"),
        P(("groups", "cell"), None),
        P(("groups", "cell"), None, None),
        P(("groups", "cell")),
        P(("gene", "cell"), None),
        P(("gene", "cell"), None),
        P(("gene", "cell"), None),
        P(None, "gene"),
        P("gene"),
    )
    return jax.shard_map(
        shards,
        mesh=mesh,
        in_specs=placed,
        out_specs=(P(("groups", "gene", "cell"), None), P(("groups", "gene", "cell"), None)),
        check_vma=False,
    )
```

profile of v0, /device:TPU:5, one launch (start us, length us, event | category | flops | bytes accessed | tf_op | source)
XLA Modules:
  0.0 559.7 jit_solution(7980614897576591471)
XLA Ops:
  7.2 0.0 copy-start
  7.2 0.0 reduce-scatter.4.cloned.1.call-start
  7.2 1.7 copy.27
  8.9 4.9 all_to_all.32
  13.8 0.5 copy.28
  14.3 10.3 %fusion.7 = f32[4096,256]{1,0:T(8,128)} fusion(bf16[2048,4096]{1,0:T(8,128)(2,1)} %param.15, bf16[256,2048]{1,0:T(8,128)(2,1)S(1)} %bitcast.44), kind=kOutput, calls=%fused_computation.25 | convolution fusion | flops 4294967296 | bytes 22020096 | tf_op jit(solution)/shard_map/dot_general | solution.py:17
  24.7 0.0 reduce-scatter.4.cloned.1.call-update
  24.7 0.0 all-gather.5.cloned.1.call-start
  24.7 0.8 copy-done.4
  25.5 1.9 all_gather.16
  27.4 69.7 %reduce-scatter.4.cloned.1.call-done = f32[256,256]{1,0:T(8,128)} async-done(((f32[4096,256]{1,0:T(8,128)}), f32[256,256]{1,0:T(8,128)}) %reduce-scatter.4.cloned.1.call-update) | async-done | bytes 262160 | tf_op jit(solution)/shard_map/reduce_scatter | solution.py:120
  97.2 1.0 fusion.1
  98.2 0.1 copy.29
  98.3 0.2 fusion
  98.6 0.3 copy.31
  98.9 0.8 reshape.62
  99.7 0.0 all-gather.5.cloned.1.call-update
  99.7 0.6 reduce-scatter.6.cloned.1.call-start
  100.3 0.3 bitcast_convert_fusion
  100.6 4.4 add.59
  105.0 6.1 %add.60 = f32[512,2048]{1,0:T(8,128)} reshape(f32[256,2,2048]{2,1,0:T(2,128)} %add.59) | data formatting | bytes 8388608 | tf_op jit(solution)/shard_map/add | solution.py:69
  111.1 42.4 %all-gather.5.cloned.1.call-done = bf16[4096,512]{0,1:T(8,128)(2,1)} async-done(((bf16[256,512]{0,1:T(8,128)(2,1)}), bf16[4096,512]{0,1:T(8,128)(2,1)}) %all-gather.5.cloned.1.call-update) | async-done | bytes 4194320 | tf_op jit(solution)/shard_map/all_gather | solution.py:131
  153.5 14.3 %add_convert_fusion.1 = bf16[512,2048]{1,0:T(8,128)(2,1)S(1)} fusion(f32[512,2048]{1,0:T(8,128)} %add.60, bf16[4096,512]{0,1:T(8,128)(2,1)} %all-gather.5.cloned.1.call-done, bf16[2048,4096]{1,0:T(8,128)(2,1)} %param.16), kind=kOutput, calls=%fused_computation.6 | convolution fusion | flops 8592031744 | bytes 27262976 | tf_op jit(solution)/shard_map/dot_general | solution.py:17
  167.8 1.3 copy-done.2
  169.1 14.5 %convolution_bitcast_fusion.1 = f32[4096,512]{0,1:T(8,128)} fusion(bf16[512,2048]{1,0:T(8,128)(2,1)S(1)} %add_convert_fusion.1, bf16[2048,4096]{1,0:T(8,128)(2,1)} %param.17), kind=kOutput, calls=%fused_computation.3 | convolution fusion | flops 8589934592 | bytes 27262976 | tf_op jit(solution)/shard_map/dot_general | solution.py:17
  183.6 0.0 reduce-scatter.6.cloned.1.call-update
  183.6 0.0 all-gather.7.cloned.1.call-start
  183.7 0.6 copy-done.7
  184.3 0.1 dynamic_slice.7
  184.3 1.8 all-gather
  186.1 0.1 broadcast_in_dim.2
  186.2 0.1 neg.22
  186.3 100.1 %reduce-scatter.6.cloned.1.call-done = f32[256,512]{0,1:T(8,128)} async-done(((f32[4096,512]{0,1:T(8,128)}), f32[256,512]{0,1:T(8,128)}) %reduce-scatter.6.cloned.1.call-update) | async-done | bytes 524304 | tf_op jit(solution)/shard_map/reduce_scatter | solution.py:134
  286.4 2.0 multiply_convert_fusion
  288.4 0.0 all-gather.7.cloned.1.call-update
  288.4 0.0 reduce-scatter.8.cloned.1.call-start
  288.5 0.5 convolution_convert_fusion.1
  288.9 0.1 copy.39
  289.1 5.0 all_to_all.33
  294.0 0.2 convert_element_type.75
  294.3 4.4 sub.18
  298.7 6.0 %sub.19 = f32[512,2048]{1,0:T(8,128)} reshape(f32[256,2,2048]{2,1,0:T(2,128)} %sub.18) | data formatting | bytes 8388608 | tf_op jit(solution)/shard_map/sub | solution.py:94
  304.8 0.1 mul.92
  304.9 0.1 mul.93
  305.0 5.4 reshape.63
  310.4 8.6 %reduce_sum.18 = f32[256,2048]{1,0:T(8,128)} reduce(f32[256,2,2048]{2,1,0:T(2,128)} %reshape.63, f32[]{:T(128)} %constant.7.clone.1), dimensions={1}, to_apply=%region_1.2 | reduce | flops 524288 | bytes 6291460 | tf_op jit(solution)/shard_map/reduce_sum | solution.py:89
  319.0 1.8 broadcast_multiply_fusion
  320.8 4.4 add.65
  325.3 6.1 %add.66 = f32[512,2048]{1,0:T(8,128)} reshape(f32[256,2,2048]{2,1,0:T(2,128)} %add.65) | data formatting | bytes 8388608 | tf_op jit(solution)/shard_map/add | solution.py:94
  331.3 10.7 %all-gather.7.cloned.1.call-done = bf16[4096,512]{0,1:T(8,128)(2,1)} async-done(((bf16[256,512]{0,1:T(8,128)(2,1)}), bf16[4096,512]{0,1:T(8,128)(2,1)}) %all-gather.7.cloned.1.call-update) | async-done | bytes 4194320 | tf_op jit(solution)/shard_map/all_gather | solution.py:146
  342.0 17.1 %add_convert_fusion = bf16[512,2048]{1,0:T(8,128)(2,1)} fusion(f32[512,2048]{1,0:T(8,128)} %sub.19, f32[512,2048]{1,0:T(8,128)} %add.66, bf16[4096,512]{0,1:T(8,128)(2,1)} %all-gather.7.cloned.1.call-done, bf16[2048,4096]{1,0:T(8,128)(2,1)} %param.17, f32[512]{0:T(512)S(1)} %mul.93, bf16[512,2048]{1,0:T(8,128)(2,1)} %copy-done.2), kind=kOutput, calls=%fused_computation.5 | convolution fusion | flops 8597274624 | bytes 33556480 | tf_op jit(solution)/shard_map/dot_general | solution.py:17
  359.2 15.0 %convolution_bitcast_fusion = f32[4096,512]{0,1:T(8,128)} fusion(bf16[512,2048]{1,0:T(8,128)(2,1)} %add_convert_fusion, bf16[2048,4096]{1,0:T(8,128)(2,1)} %param.16), kind=kOutput, calls=%fused_computation.2 | convolution fusion | flops 8589934592 | bytes 27262976 | tf_op jit(solution)/shard_map/dot_general | solution.py:17
  374.2 0.0 reduce-scatter.8.cloned.1.call-update
  374.2 0.0 all-gather.9.cloned.1.call-start
  374.2 102.7 %reduce-scatter.8.cloned.1.call-done = f32[256,512]{0,1:T(8,128)} async-done(((f32[4096,512]{0,1:T(8,128)}), f32[256,512]{0,1:T(8,128)}) %reduce-scatter.8.cloned.1.call-update) | async-done | bytes 524304 | tf_op jit(solution)/shard_map/reduce_scatter | solution.py:150
  477.0 1.3 reshape.64
  478.3 0.6 reduce_sum.19
  478.9 0.1 copy.33
  479.1 0.8 multiply_convert_fusion.1
  479.8 0.0 all-gather.9.cloned.1.call-update
  479.9 15.3 %convolution_convert_fusion = bf16[2048,4096]{1,0:T(8,128)(2,1)} fusion(bf16[512,2048]{1,0:T(8,128)(2,1)} %add_convert_fusion, bf16[4096,512]{0,1:T(8,128)(2,1)} %all-gather.5.cloned.1.call-done), kind=kOutput, calls=%fused_computation.1 | convolution fusion | flops 8598323200 | bytes 23068672 | tf_op jit(solution)/shard_map/dot_general | solution.py:17
  495.2 26.4 %all-gather.9.cloned.1.call-done = bf16[4096,256]{1,0:T(8,128)(2,1)} async-done(((bf16[256,256]{1,0:T(8,128)(2,1)}), bf16[4096,256]{1,0:T(8,128)(2,1)}) %all-gather.9.cloned.1.call-update) | async-done | bytes 2097168 | tf_op jit(solution)/shard_map/all_gather | solution.py:161
  521.6 9.7 %convert_bitcast_fusion = bf16[2048,4096]{0,1:T(8,128)(2,1)} fusion(bf16[4096,256]{1,0:T(8,128)(2,1)} %all-gather.9.cloned.1.call-done, bf16[256,2048]{1,0:T(8,128)(2,1)S(1)} %bitcast.45), kind=kOutput, calls=%fused_computation | convolution fusion | flops 4303355904 | bytes 19922944 | tf_op jit(solution)/shard_map/dot_general | solution.py:17
  531.3 21.3 %copy.34 = bf16[2048,4096]{1,0:T(8,128)(2,1)} copy(bf16[2048,4096]{0,1:T(8,128)(2,1)} %convert_bitcast_fusion) | data formatting | bytes 33554432
  (16 shorter events, 0.0 us)
Async XLA Ops:
  7.2 281.3 %copy-start = (bf16[128,4096]{1,0:T(8,128)(2,1)S(1)}, bf16[128,4096]{1,0:T(8,128)(2,1)}, u32[]{:S(2)}) copy-start(bf16[128,4096]{1,0:T(8,128)(2,1)} %param.11) | copy-start | bytes 3145732
  7.2 90.0 %reduce-scatter.4.cloned.1.call-start = ((), (), s32[]{:S(2)}) async-start(), calls=%async_computation.5 | async-start | bytes 4456448 | tf_op jit(solution)/shard_map/reduce_scatter | solution.py:120
  24.7 0.8 copy-start.4
  24.7 73.7 %copy-start.5 = (bf16[128,512]{1,0:T(8,128)(2,1)S(1)}, bf16[128,512]{1,0:T(8,128)(2,1)}, u32[]{:S(2)}) copy-start(bf16[128,512]{1,0:T(8,128)(2,1)} %param.18) | copy-start | bytes 393220
  24.7 128.8 %all-gather.5.cloned.1.call-start = ((), (), s32[]{:S(2)}) async-start(), calls=%async_computation.6 | async-start | bytes 4456448 | tf_op jit(solution)/shard_map/all_gather | solution.py:131
  99.7 186.7 %reduce-scatter.6.cloned.1.call-start = ((), (), s32[]{:S(2)}) async-start(), calls=%async_computation.7 | async-start | bytes 8912896 | tf_op jit(solution)/shard_map/reduce_scatter | solution.py:134
  167.8 1.3 copy-start.2
  183.6 0.7 copy-start.7
  183.6 0.8 copy-start.8
  183.6 104.9 %copy-start.6 = (s32[1,128]{1,0:T(1,128)S(1)}, s32[1,128]{1,0:T(1,128)}, u32[]{:S(2)}) copy-start(s32[1,128]{1,0:T(1,128)} %param.12) | copy-start | bytes 1540
  183.6 158.4 %all-gather.7.cloned.1.call-start = ((), (), s32[]{:S(2)}) async-start(), calls=%async_computation.8 | async-start | bytes 4456448 | tf_op jit(solution)/shard_map/all_gather | solution.py:146
  288.4 188.6 %reduce-scatter.8.cloned.1.call-start = ((), (), s32[]{:S(2)}) async-start(), calls=%async_computation.9 | async-start | bytes 8912896 | tf_op jit(solution)/shard_map/reduce_scatter | solution.py:150
  374.2 104.9 %copy-start.3 = (f32[256,256]{1,0:T(8,128)S(1)}, f32[256,256]{1,0:T(8,128)}, u32[]{:S(2)}) copy-start(f32[256,256]{1,0:T(8,128)} %reduce-scatter.4.cloned.1.call-done) | copy-start | bytes 786436
  374.2 147.4 %all-gather.9.cloned.1.call-start = ((), (), s32[]{:S(2)}) async-start(), calls=%async_computation.10 | async-start | bytes 2228224 | tf_op jit(solution)/shard_map/all_gather | solution.py:161
  531.3 21.3 %copy-start.1 = (bf16[128,4096]{1,0:T(8,128)(2,1)S(1)}, bf16[128,4096]{1,0:T(8,128)(2,1)}, u32[]{:S(2)}) copy-start(bf16[128,4096]{1,0:T(8,128)(2,1)} %param.11) | copy-start | bytes 3145732
Sparse Core Ops, SparseCore 0:
  24.8 72.3 reduce-scatter.3
  99.8 53.6 all-gather.4
  183.7 102.6 reduce-scatter.5
  288.6 53.3 all-gather.6
  374.3 102.6 reduce-scatter.7
  480.0 41.5 all-gather.8
where the time goes:
time: 566 us; the launch traced here: 560 us
  waiting for transfers between devices  352 us (62%)
  matrix products  96.9 us (17%)
  local copies, waits for them, and re-layouts  66.5 us (12%)
  other arithmetic  15.3 us (3%)
  between operations  14.6 us (3%)
  blocking collectives  13.5 us (2%)
    reduce_scatter x1, waiting for transfers between devices, spread_lat(): lax.psum_scatter(producer(jnp.int32(0), n_rows // lax.axis_size(('gene',...  103 us
    reduce_scatter x1, waiting for transfers between devices, spread_crit(): lax.psum_scatter(producer(jnp.int32(0), n_rows // lax.axis_size(('gene',...  100 us
    dot_general x8, matrix products, contract(): lax.dot_general(former, latter, (((former_dim,), (latter_dim,)), ((), ())...  96.4 us
    reduce_scatter x1, waiting for transfers between devices, spread_enc(): lax.psum_scatter(producer(jnp.int32(0), n_rows // lax.axis_size(('gene',...  69.7 us
    all_gather x1, waiting for transfers between devices, gather_lat(): return lax.all_gather(latent_share, ('gene', 'cell'), axis=0, tiled=True)  42.4 us
    all_gather x1, waiting for transfers between devices, map_enc(): lax.all_gather(enc_grad, ('gene', 'cell'), axis=0, tiled=True)  26.4 us
    unnamed x21, local copies, waits for them, and re-layouts  25.7 us
  transfers between devices with their start and end apart: 6, of which 6 were waited for; matrix products, arithmetic and copies ran while one was open for 11% of the time, Pallas kernels for 0%

commit v1 on v0

v1 whole, which is shorter than its diff:
```python
import functools
import math

import jax
import jax.numpy as jnp
from jax import lax
from jax.experimental import pallas as pl
from jax.experimental.pallas import tpu as pltpu
from jax.sharding import PartitionSpec as P

G = 32768
MESH = pl.DeviceIdType.MESH
F32 = jnp.float32
BF16 = jnp.bfloat16


def silu_grad(inputs):
    sigmoid = 1.0 / (1.0 + jnp.exp(-inputs))
    return sigmoid * (1.0 + inputs * (1.0 - sigmoid))


def contract(former, latter, former_dim, latter_dim):
    return lax.dot_general(
        former,
        latter,
        (((former_dim,), (latter_dim,)), ((), ())),
        preferred_element_type=F32,
    )


def row_loop(n_rows, tile, body):
    def step(i, carry):
        body(pl.ds(pl.multiple_of(i * tile, tile), tile), pl.multiple_of(i * tile, tile))
        return carry

    lax.fori_loop(0, n_rows // tile, step, 0)


def exchange_kernel(kind, nz, nx, nch, *refs):
    if kind == "enc":
        p_ref, g_ref, e_ref = refs[:3]
        rest = refs[3:]
    elif kind == "crit":
        p_ref, weight_ref, readout_ref, g_ref = refs[:4]
        rest = refs[4:]
    else:
        p_ref, e_ref, g_ref = refs[:3]
        rest = refs[3:]
    (c_buf, s1_buf, x_buf, s2_buf, z_buf) = rest[:5]
    sems = rest[5:]
    cs_send, cs_recv, xs_send, xs_recv, zs_send, zs_recv = sems[:6]
    zg_send, zg_recv, xg_send, xg_recv, cg_send, cg_recv = sems[6:]

    n_rows, hidden = p_ref.shape
    half = hidden // 2
    quarter = half // nx
    width = quarter // nch
    z_rows = n_rows // nz
    group = lax.axis_index("groups")
    gene = lax.axis_index("gene")
    core = lax.axis_index("cell")
    z = gene // nx
    x = gene % nx
    other = (group, gene, 1 - core)

    def x_peer(offset):
        return (group, z * nx + (x + offset) % nx, core)

    def z_peer(offset):
        return (group, ((z + offset) % nz) * nx + x, core)

    def cols(which, block, k):
        return pl.ds(pl.multiple_of(which * half + block * quarter + k * width, 128), width)

    def part(k):
        return pl.ds(k * width, width)

    def z_block(which):
        return pl.ds(pl.multiple_of(which * z_rows, 16), z_rows)

    barrier = pltpu.get_barrier_semaphore()
    peers = [other] + [x_peer(o) for o in range(1, nx)] + [z_peer(o) for o in range(1, nz)]
    for peer in peers:
        pl.semaphore_signal(barrier, inc=1, device_id=peer, device_id_type=MESH)
    pl.semaphore_wait(barrier, len(peers))

    def remote(src, dst, send, recv, peer):
        copy = pltpu.make_async_remote_copy(
            src_ref=src,
            dst_ref=dst,
            send_sem=send,
            recv_sem=recv,
            device_id=peer,
            device_id_type=MESH,
        )
        copy.start()
        return copy

    started = {}

    def stage0(k):
        started["c", k] = [
            remote(
                p_ref.at[:, cols(1 - core, (x + o) % nx, k)],
                c_buf.at[o, :, part(k)],
                cs_send.at[k, o],
                cs_recv.at[k, o],
                other,
            )
            for o in list(range(1, nx)) + [0]
        ]

    def stage1(k):
        for copy in started["c", k]:
            copy.wait_recv()
        for o in range(1, nx):
            mine = cols(core, (x + o) % nx, k)

            def add(rows, _):
                s1_buf[o - 1, rows, part(k)] = (
                    p_ref[rows, mine].astype(F32) + c_buf[o, rows, part(k)].astype(F32)
                ).astype(BF16)

            row_loop(n_rows, 32, add)
        started["x", k] = [
            remote(
                s1_buf.at[o - 1, :, part(k)],
                x_buf.at[o - 1, :, part(k)],
                xs_send.at[k, o - 1],
                xs_recv.at[k, o - 1],
                x_peer(o),
            )
            for o in range(1, nx)
        ]

    def stage2(k):
        for copy in started["x", k]:
            copy.wait_recv()
        mine = cols(core, x, k)

        def add(rows, _):
            total = p_ref[rows, mine].astype(F32) + c_buf[0, rows, part(k)].astype(F32)
            for o in range(1, nx):
                total = total + x_buf[o - 1, rows, part(k)].astype(F32)
            s2_buf[rows, part(k)] = total.astype(BF16)

        row_loop(n_rows, 32, add)
        started["z", k] = [
            remote(
                s2_buf.at[z_block((z + o) % nz), part(k)],
                z_buf.at[o - 1, :, part(k)],
                zs_send.at[k, o - 1],
                zs_recv.at[k, o - 1],
                z_peer(o),
            )
            for o in range(1, nz)
        ]

    def stage3(k):
        for copy in started["z", k]:
            copy.wait_recv()
        mine = cols(core, x, k)

        def finish(rows, start):
            own = pl.ds(pl.multiple_of(z * z_rows + start, 16), 16)
            total = p_ref[own, mine].astype(F32) + c_buf[0, own, part(k)].astype(F32)
            for o in range(1, nx):
                total = total + x_buf[o - 1, own, part(k)].astype(F32)
            for o in range(1, nz):
                total = total + z_buf[o - 1, rows, part(k)].astype(F32)
            if kind == "enc":
                e_ref[rows, part(k)] = total
                value = total / (1.0 + jnp.exp(-total))
            elif kind == "crit":
                value = -weight_ref[own, :] * readout_ref[:, mine] * silu_grad(total)
            else:
                value = silu_grad(e_ref[rows, part(k)]) * total
            g_ref[own, mine] = value.astype(BF16)

        row_loop(z_rows, 16, finish)
        block = g_ref.at[z_block(z), mine]
        started["zg", k] = [
            remote(block, block, zg_send.at[k, o - 1], zg_recv.at[k, o - 1], z_peer(o))
            for o in range(1, nz)
        ]

    def stage4(k):
        for copy in started["zg", k]:
            copy.wait_recv()
        block = g_ref.at[:, cols(core, x, k)]
        started["xg", k] = [
            remote(block, block, xg_send.at[k, o - 1], xg_recv.at[k, o - 1], x_peer(o))
            for o in range(1, nx)
        ]
        started["cg", k] = [remote(block, block, cg_send.at[k, 0], cg_recv.at[k, 0], other)]

    def stage5(k):
        for o, copy in enumerate(started["xg", k], 1):
            copy.wait_recv()
            block = g_ref.at[:, cols(core, (x + nx - o) % nx, k)]
            started["cg", k].append(
                remote(block, block, cg_send.at[k, o], cg_recv.at[k, o], other)
            )

    def stage6(k):
        for copy in started["cg", k]:
            copy.wait_recv()

    stages = (stage0, stage1, stage2, stage3, stage4, stage5, stage6)
    for k in range(nch):
        stage0(k)
    for step in range(1, nch + len(stages) - 1):
        for index in range(len(stages) - 1, 0, -1):
            if 0 <= step - index < nch:
                stages[index](step - index)
    for copies in started.values():
        for copy in copies:
            copy.wait_send()


def exchange(kind, partial, extras, n_gene):
    nx = 2 if n_gene <= 8 else 4
    nz = n_gene // nx
    n_rows, hidden = partial.shape
    quarter = hidden // (2 * nx)
    nch = min(4, quarter // 128)
    gathered = jax.ShapeDtypeStruct((n_rows, hidden), BF16)
    vmem = pl.BlockSpec(memory_space=pltpu.VMEM)
    if kind == "enc":
        out_shape = (gathered, jax.ShapeDtypeStruct((n_rows // nz, quarter), F32))
        out_specs = (vmem, vmem)
    else:
        out_shape, out_specs = gathered, vmem
    dma = pltpu.SemaphoreType.DMA
    counts = (nx, nx, nx - 1, nx - 1, nz - 1, nz - 1, nz - 1, nz - 1, nx - 1, nx - 1, nx, nx)
    return pl.pallas_call(
        functools.partial(exchange_kernel, kind, nz, nx, nch),
        out_shape=out_shape,
        in_specs=[vmem] * (1 + len(extras)),
        out_specs=out_specs,
        scratch_shapes=[
            pltpu.VMEM((nx, n_rows, quarter), BF16),
            pltpu.VMEM((nx - 1, n_rows, quarter), BF16),
            pltpu.VMEM((nx - 1, n_rows, quarter), BF16),
            pltpu.VMEM((n_rows, quarter), BF16),
            pltpu.VMEM((nz - 1, n_rows // nz, quarter), BF16),
        ]
        + [dma((nch, count)) for count in counts],
        compiler_params=pltpu.CompilerParams(
            collective_id={"enc": 0, "crit": 1, "lat": 2}[kind],
            has_side_effects=True,
            vmem_limit_bytes=40 * 1024 * 1024,
        ),
    )(partial, *extras)


def paired_rows(perturbed, pair_index):
    per_block = pair_index.shape[1]
    one_hot = (
        pair_index.reshape(per_block)[:, None] == jnp.arange(per_block, dtype=jnp.int32)[None, :]
    ).astype(perturbed.dtype)
    return jnp.dot(one_hot, perturbed, preferred_element_type=F32).astype(perturbed.dtype)


def shards(
    control, perturbed, pair_index, noise_draws, cell_mass, w_enc, w_dec, w_crit, w_noise, readout
):
    n_gene = lax.axis_size("gene")
    n_draws = noise_draws.shape[1]
    control_all = lax.all_to_all(control, "cell", split_axis=1, concat_axis=0, tiled=True)
    n_cells, n_genes = control_all.shape
    n_pairs = n_cells * n_draws
    hidden = w_enc.shape[1]
    w_noise_all = lax.all_gather(w_noise, "gene", axis=1, tiled=True)
    readout_all = lax.all_gather(readout, "gene", axis=0, tiled=True)
    noise_all = lax.all_gather(noise_draws.transpose(1, 0, 2), "cell", axis=1, tiled=True)
    mass_all = lax.all_gather(cell_mass, "cell", axis=0, tiled=True)
    target = lax.all_to_all(
        paired_rows(perturbed, pair_index), "cell", split_axis=1, concat_axis=0, tiled=True
    )

    enc_part = contract(control_all, w_enc, 1, 0).astype(BF16)
    silu_enc, enc_own = exchange("enc", enc_part, (), n_gene)
    shift = contract(noise_all.reshape(n_pairs, noise_all.shape[2]), w_noise_all, 1, 0)
    latent = (
        (silu_enc.astype(F32)[None] + shift.reshape(n_draws, n_cells, hidden))
        .astype(BF16)
        .reshape(n_pairs, hidden)
    )
    decoded = contract(latent, w_dec, 1, 1).reshape(n_draws, n_cells, n_genes)
    moved = (control_all.astype(F32)[None] + decoded).astype(BF16)
    crit_part = contract(moved.reshape(n_pairs, n_genes), w_crit, 1, 0).astype(BF16)
    weight = jnp.tile(8.0 / n_draws * mass_all, n_draws)[:, None]
    critic_grad = exchange("crit", crit_part, (weight, readout_all[None, :]), n_gene)
    critic_back = contract(critic_grad, w_crit, 1, 1).reshape(n_draws, n_cells, n_genes)
    moved_f32 = moved.astype(F32)
    mean_moved = jnp.sum(moved_f32, axis=0) / n_draws
    cost_grad = (
        8.0
        / (n_draws * math.sqrt(G))
        * mass_all[None, :, None]
        * (0.5 * moved_f32 + (0.5 * mean_moved - target.astype(F32))[None])
    )
    moved_grad = (cost_grad + critic_back).astype(BF16)
    summed = jnp.sum(moved_grad.astype(F32), axis=0).astype(BF16)
    lat_part = contract(summed, w_dec, 1, 0).astype(BF16)
    enc_grad = exchange("lat", lat_part, (enc_own,), n_gene)
    grad_dec = contract(moved_grad.reshape(n_pairs, n_genes), latent, 0, 0).astype(BF16)
    grad_enc = contract(control_all, enc_grad, 0, 0).astype(BF16)
    return (grad_enc, grad_dec)


def solution(mesh):
    placed = (
        P(("groups", "cell"), "gene"),
        P(("groups", "cell"), "gene"),
        P(("groups", "cell"), None),
        P(("groups", "cell"), None, None),
        P(("groups", "cell")),
        P(("gene", "cell"), None),
        P(("gene", "cell"), None),
        P(("gene", "cell"), None),
        P(None, "gene"),
        P("gene"),
    )
    return jax.shard_map(
        shards,
        mesh=mesh,
        in_specs=placed,
        out_specs=(P(("groups", "gene", "cell"), None), P(("groups", "gene", "cell"), None)),
        check_vma=False,
    )
```

time: 566 us -> 345 us (0.61)
  waiting for transfers between devices: 352 us -> 0.72 us
  Pallas kernels: 0 us -> 166 us
  local copies, waits for them, and re-layouts: 66.5 us -> 26.4 us
  blocking collectives: 13.5 us -> 29.5 us
  matrix products: 96.9 us -> 89 us
  starting transfers between devices: 0.77 us -> 7.85 us
    reduce_scatter x3 -> x0, waiting for transfers between devices: 273 us -> none  [the longest x1 103 us: spread_lat(): lax.psum_scatter(producer(jnp.int32(0), n_rows // lax.axis_size(('gene',...]
    pallas_call x0 -> x3, Pallas kernels: none -> 166 us  [exchange(): pl.pallas_call(functools.partial(exchange_kernel, kind, nz, nx, nch), out...]
    all_gather x3 -> x1, waiting for transfers between devices: 79.5 us -> 0.01 us  [shards(): w_noise_all = lax.all_gather(w_noise, 'gene', axis=1, tiled=True)]
    all_gather x2 -> x3, blocking collectives: 3.67 us -> 29.5 us  [the longest x1 21.5 us: shards(): readout_all = lax.all_gather(readout, 'gene', axis=0, tiled=True)]
    add x4 -> x0, local copies, waits for them, and re-layouts: 21 us -> none  [the longest x2 10.5 us: train_step(): control.astype(jnp.float32)[:, None, :] + decoded]
    sub x2 -> x0, local copies, waits for them, and re-layouts: 10.5 us -> none  [train_step(): 0.5 * moved_f32 + 0.5 * mean_moved - target.astype(jnp.float32)[:, None, :]]
    all_to_all x2 -> x0, blocking collectives: 9.87 us -> none  [the longest x1 5 us: shards(): lax.all_to_all(target, 'cell', split_axis=1, concat_axis=0, tiled=True)]
    dot_general x8, matrix products: 96.4 us -> 88.6 us  [contract(): lax.dot_general(former, latter, (((former_dim,), (latter_dim,)), ((), ())...]
  transfers between devices with their start and end apart: 6 -> 3, of which waited for: 6 -> 0; matrix products, arithmetic and copies ran while one was open for 11% -> 18% of each run, Pallas kernels for 0% -> 36%
where the time goes in v1:
time: 345 us; the launch traced here: 344 us
  Pallas kernels  166 us (48%)
  matrix products  89 us (26%)
  blocking collectives  29.5 us (9%)
  local copies, waits for them, and re-layouts  26.4 us (8%)
  between operations  14.2 us (4%)
  other arithmetic  10.3 us (3%)
  starting transfers between devices  7.85 us (2%)
    pallas_call x3, Pallas kernels, exchange(): pl.pallas_call(functools.partial(exchange_kernel, kind, nz, nx, nch), out...  166 us
    dot_general x8, matrix products, contract(): lax.dot_general(former, latter, (((former_dim,), (latter_dim,)), ((), ())...  88.6 us
    unnamed x26, local copies, waits for them, and re-layouts  24.1 us
    all_gather x1, blocking collectives, shards(): readout_all = lax.all_gather(readout, 'gene', axis=0, tiled=True)  21.5 us
  transfers between devices with their start and end apart: 3, of which 0 were waited for; matrix products, arithmetic and copies ran while one was open for 18% of the time, Pallas kernels for 36%

profile of v1, /device:TPU:5, one launch (start us, length us, event | category | flops | bytes accessed | tf_op | source)
XLA Modules:
  0.0 344.2 jit_solution(11053243052255197691)
XLA Ops:
  7.2 0.0 copy-start
  7.2 0.0 copy-start.8
  7.2 1.7 copy.28
  8.9 1.3 copy.29
  10.2 4.2 %all-to-all-start = ((bf16[128,2,2048]{2,0,1:T(8,128)(2,1)}), bf16[128,2,2048]{2,0,1:T(8,128)(2,1)S(1)}, u32[]{:S(2)}, u32[]{:S(2)}) async-start(bf16[128,2,2048]{2,0,1:T(8,128)(2,1)} %copy.29), calls=%async_computation | async-start | bytes 2097152 | tf_op jit(solution)/shard_map/all_to_all | solution.py:270
  14.5 0.0 all-gather.4.cloned.1.call-start
  14.5 0.7 all-gather.4.cloned.1.call-update
  15.2 0.0 copy-done
  15.2 0.0 copy-done.8
  15.2 0.5 convolution_convert_fusion.3
  15.7 1.0 copy.41
  16.7 0.0 all-to-all-done
  16.7 0.0 copy-start.2
  16.7 3.6 %all-to-all-start.1 = ((bf16[128,2,2048]{2,0,1:T(8,128)(2,1)}), bf16[128,2,2048]{2,0,1:T(8,128)(2,1)S(1)}, u32[]{:S(2)}, u32[]{:S(2)}) async-start(bf16[128,2,2048]{2,0,1:T(8,128)(2,1)} %bitcast.56), calls=%async_computation.1 | async-start | bytes 2097152 | tf_op jit(solution)/shard_map/all_to_all | solution.py:278
  20.3 8.4 %convolution_convert_fusion.2.refs_0_ = bf16[256,4096]{1,0:T(8,128)(2,1)S(1)} fusion(bf16[256,2048]{1,0:T(8,128)(2,1)S(1)} %bitcast.60, bf16[2048,4096]{1,0:T(8,128)(2,1)} %param.15), kind=kOutput, calls=%fused_computation.9 | convolution fusion | flops 4296015872 | bytes 19922944 | tf_op jit(solution)/shard_map/dot_general | solution.py:23
  28.8 0.0 copy-start.6
  28.8 0.0 copy-start.9
  28.8 0.0 copy-start.7
  28.8 53.3 %shard_map.113 = (bf16[256,4096]{1,0:T(8,128)(2,1)S(1)}, f32[64,1024]{1,0:T(8,128)S(1)}) custom-call(bf16[256,4096]{1,0:T(8,128)(2,1)S(1)} %convolution_convert_fusion.2.refs_0_), custom_call_target="tpu_custom_call" | custom-call | tf_op jit(solution)/shard_map/pallas_call | solution.py:236
  82.1 2.5 convert_element_type.61
  84.6 0.0 copy-done.6
  84.6 0.0 copy-done.9
  84.6 1.8 all-gather
  86.4 0.1 copy.38
  86.6 0.0 copy-done.7
  86.6 21.5 %all-gather.1 = f32[8,1,512]{2,1,0:T(1,128)S(1)} all-gather(f32[1,1,512]{2,1,0:T(1,128)S(1)} %bitcast.70), channel_id=1, replica_groups=mesh['groups'=2,'gene'=8,'cell'=2] {'gene'}, dimensions={0}, use_global_device_ids=true | all-gather | bytes 18432 | tf_op jit(solution)/shard_map/all_gather | solution.py:275
  108.1 6.2 %all_gather.13 = bf16[2,256,128]{2,1,0:T(8,128)(2,1)S(1)} all-gather(bf16[2,128,128]{2,1,0:T(8,128)(2,1)S(1)} %bitcast.66), channel_id=1, replica_groups=mesh['groups'=2,'gene'=8,'cell'=2] {'cell'}, dimensions={1}, use_global_device_ids=true | all-gather | bytes 196608 | tf_op jit(solution)/shard_map/all_gather | solution.py:276
  114.3 0.0 copy-done.2
  114.3 1.6 bitcast_convert_fusion.1
  116.0 0.0 all-gather.4.cloned.1.call-done
  116.0 3.8 %add_convert_fusion = bf16[2,256,4096]{2,1,0:T(8,128)(2,1)S(1)} fusion(bf16[2,256,128]{2,1,0:T(8,128)(2,1)S(1)} %all_gather.13, f32[256,4096]{1,0:T(8,128)} %convert_element_type.61, bf16[128,4096]{1,0:T(8,128)(2,1)} %all-gather.4.cloned.1.call-done), kind=kOutput, calls=%fused_computation.4 | convolution fusion | flops 541065216 | bytes 9568256 | tf_op jit(solution)/shard_map/dot_general | solution.py:23
  119.7 0.0 copy-start.4
  119.7 16.6 %convert_reduce_fusion = (f32[256,2048]{1,0:T(8,128)}, bf16[2,256,2048]{2,1,0:T(8,128)(2,1)}) fusion(bf16[2,256,4096]{2,1,0:T(8,128)(2,1)S(1)} %add_convert_fusion, bf16[2048,4096]{1,0:T(8,128)(2,1)} %param.16, f32[256,2048]{1,0:T(8,128)} %bitcast_convert_fusion.1), kind=kOutput, calls=%fused_computation.6 | convolution fusion | flops 8593604608 | bytes 27262976 | tf_op jit(solution)/shard_map/dot_general | solution.py:23
  136.3 0.0 copy-done.4
  136.3 13.0 %convolution_convert_fusion.refs_0_ = bf16[512,4096]{1,0:T(8,128)(2,1)S(1)} fusion(bf16[512,2048]{1,0:T(8,128)(2,1)} %bitcast.65, bf16[2048,4096]{1,0:T(8,128)(2,1)} %param.17), kind=kOutput, calls=%fused_computation.5 | convolution fusion | flops 8592031744 | bytes 23068672 | tf_op jit(solution)/shard_map/dot_general | solution.py:23
  149.3 69.5 %shard_map.114 = bf16[512,4096]{1,0:T(8,128)(2,1)S(1)} custom-call(bf16[512,4096]{1,0:T(8,128)(2,1)S(1)} %convolution_convert_fusion.refs_0_, f32[512,1]{1,0:T(8,128)S(1)} %bitcast.58, f32[1,4096]{1,0:T(1,128)S(1)} %bitcast.59), custom_call_target="tpu_custom_call" | custom-call | tf_op jit(solution)/shard_map/pallas_call | solution.py:236
  218.9 13.8 %fusion.12 = f32[512,2048]{1,0:T(8,128)} fusion(bf16[512,4096]{1,0:T(8,128)(2,1)S(1)} %shard_map.114, bf16[2048,4096]{1,0:T(8,128)(2,1)} %param.17), kind=kOutput, calls=%fused_computation.27 | convolution fusion | flops 8589934592 | bytes 25165824 | tf_op jit(solution)/shard_map/dot_general | solution.py:23
  232.6 0.0 all-to-all-done.1
  232.6 0.0 copy-start.3
  232.6 2.0 bitcast_subtract_fusion
  234.7 0.8 copy-done.3
  235.5 4.1 %fusion.10 = (bf16[256,2048]{1,0:T(8,128)(2,1)S(1)}, bf16[2,256,2048]{2,1,0:T(8,128)(2,1)}) fusion(f32[2,256,2048]{2,1,0:T(8,128)S(1)} %bitcast.62, f32[256,2048]{1,0:T(8,128)S(1)} %bitcast_subtract_fusion, bf16[2,256,2048]{2,1,0:T(8,128)(2,1)} %get-tuple-element.19, f32[256]{0:T(256)S(1)} %bitcast.68), kind=kLoop, calls=%fused_computation.26 | loop fusion | flops 6815744 | bytes 11535360 | tf_op jit(solution)/shard_map/reduce_sum | solution.py:305
  239.6 8.4 %convolution_convert_fusion.1.refs_0_ = bf16[256,4096]{1,0:T(8,128)(2,1)S(1)} fusion(bf16[256,2048]{1,0:T(8,128)(2,1)S(1)} %get-tuple-element.14, bf16[2048,4096]{1,0:T(8,128)(2,1)} %param.16), kind=kOutput, calls=%fused_computation.8 | convolution fusion | flops 4296015872 | bytes 19922944 | tf_op jit(solution)/shard_map/dot_general | solution.py:23
  248.0 43.4 %shard_map.115 = bf16[256,4096]{1,0:T(8,128)(2,1)S(1)} custom-call(bf16[256,4096]{1,0:T(8,128)(2,1)S(1)} %convolution_convert_fusion.1.refs_0_, f32[64,1024]{1,0:T(8,128)S(1)} %get-tuple-element.5.refs_1_), custom_call_target="tpu_custom_call" | custom-call | tf_op jit(solution)/shard_map/pallas_call | solution.py:236
  291.4 9.8 %convert_bitcast_fusion = bf16[2048,4096]{0,1:T(8,128)(2,1)} fusion(bf16[256,4096]{1,0:T(8,128)(2,1)S(1)} %shard_map.115, bf16[256,2048]{1,0:T(8,128)(2,1)} %bitcast.61), kind=kOutput, calls=%fused_computation.3 | convolution fusion | flops 4303355904 | bytes 19922944 | tf_op jit(solution)/shard_map/dot_general | solution.py:23
  301.2 0.0 copy-start.5
  301.2 21.3 %copy.34 = bf16[2048,4096]{1,0:T(8,128)(2,1)} copy(bf16[2048,4096]{0,1:T(8,128)(2,1)} %convert_bitcast_fusion) | data formatting | bytes 33554432
  322.5 0.0 copy-done.5
  322.5 0.0 copy-start.1
  322.5 14.8 %bitcast_convert_fusion = bf16[2048,4096]{1,0:T(8,128)(2,1)} fusion(bf16[2,256,2048]{2,1,0:T(8,128)(2,1)S(1)} %copy-done.5, bf16[2,256,4096]{2,1,0:T(8,128)(2,1)} %copy-done.4), kind=kOutput, calls=%fused_computation | convolution fusion | flops 8598323200 | bytes 23068672 | tf_op jit(solution)/shard_map/dot_general | solution.py:23
  337.4 0.0 copy-done.1
  (4 shorter events, 0.0 us)
Async XLA Ops:
  7.2 8.0 %copy-start = (bf16[128,4096]{1,0:T(8,128)(2,1)S(1)}, bf16[128,4096]{1,0:T(8,128)(2,1)}, u32[]{:S(2)}) copy-start(bf16[128,4096]{1,0:T(8,128)(2,1)} %param.11) | copy-start | bytes 3145732
  7.2 8.0 %copy-start.8 = (s32[1,128]{1,0:T(1,128)S(1)}, s32[1,128]{1,0:T(1,128)}, u32[]{:S(2)}) copy-start(s32[1,128]{1,0:T(1,128)} %param.12) | copy-start | bytes 1540
  10.2 6.5 %all-to-all-start = ((bf16[128,2,2048]{2,0,1:T(8,128)(2,1)}), bf16[128,2,2048]{2,0,1:T(8,128)(2,1)S(1)}, u32[]{:S(2)}, u32[]{:S(2)}) async-start(bf16[128,2,2048]{2,0,1:T(8,128)(2,1)} %copy.29), calls=%async_computation | async-start | bytes 2097152 | tf_op jit(solution)/shard_map/all_to_all | solution.py:270
  14.5 101.5 %all-gather.4.cloned.1.call-start = ((), (), s32[]{:S(2)}) async-start(), calls=%async_computation.2 | async-start | bytes 1179648 | tf_op jit(solution)/shard_map/all_gather | solution.py:274
  16.7 97.6 %copy-start.2 = (bf16[128,2,2048]{2,0,1:T(8,128)(2,1)}, bf16[128,2,2048]{2,0,1:T(8,128)(2,1)S(1)}, u32[]{:S(2)}) copy-start(bf16[128,2,2048]{2,0,1:T(8,128)(2,1)S(1)} %all-to-all-done) | copy-start | bytes 3145732
  16.7 215.9 %all-to-all-start.1 = ((bf16[128,2,2048]{2,0,1:T(8,128)(2,1)}), bf16[128,2,2048]{2,0,1:T(8,128)(2,1)S(1)}, u32[]{:S(2)}, u32[]{:S(2)}) async-start(bf16[128,2,2048]{2,0,1:T(8,128)(2,1)} %bitcast.56), calls=%async_computation.1 | async-start | bytes 2097152 | tf_op jit(solution)/shard_map/all_to_all | solution.py:278
  28.8 55.9 %copy-start.6 = (bf16[128,2,128]{2,1,0:T(2,128)(2,1)S(1)}, bf16[128,2,128]{2,1,0:T(2,128)(2,1)}, u32[]{:S(2)}) copy-start(bf16[128,2,128]{2,1,0:T(2,128)(2,1)} %param.13) | copy-start | bytes 196612
  28.8 55.9 %copy-start.9 = (f32[128]{0:T(128)S(1)}, f32[128]{0:T(128)}, u32[]{:S(2)}) copy-start(f32[128]{0:T(128)} %param.14) | copy-start | bytes 1540
  28.8 57.8 %copy-start.7 = (f32[512]{0:T(512)S(1)}, f32[512]{0:T(512)}, u32[]{:S(2)}) copy-start(f32[512]{0:T(512)} %param.19) | copy-start | bytes 6148
  119.7 16.6 %copy-start.4 = (bf16[2,256,4096]{2,1,0:T(8,128)(2,1)}, bf16[2,256,4096]{2,1,0:T(8,128)(2,1)S(1)}, u32[]{:S(2)}) copy-start(bf16[2,256,4096]{2,1,0:T(8,128)(2,1)S(1)} %add_convert_fusion) | copy-start | bytes 12582916
  232.6 2.8 copy-start.3
  301.2 21.3 %copy-start.5 = (bf16[2,256,2048]{2,1,0:T(8,128)(2,1)S(1)}, bf16[2,256,2048]{2,1,0:T(8,128)(2,1)}, u32[]{:S(2)}) copy-start(bf16[2,256,2048]{2,1,0:T(8,128)(2,1)} %get-tuple-element.15) | copy-start | bytes 6291460
  322.5 14.8 %copy-start.1 = (bf16[128,4096]{1,0:T(8,128)(2,1)S(1)}, bf16[128,4096]{1,0:T(8,128)(2,1)}, u32[]{:S(2)}) copy-start(bf16[128,4096]{1,0:T(8,128)(2,1)} %param.11) | copy-start | bytes 3145732
Sparse Core Ops, SparseCore 0:
  17.3 47.1 all-gather.3

commit v2 on v1

--- a/solution.py
+++ b/solution.py
@@ -38,8 +38,8 @@
 
 def exchange_kernel(kind, nz, nx, nch, *refs):
     if kind == "enc":
-        p_ref, g_ref, e_ref = refs[:3]
-        rest = refs[3:]
+        p_ref, noise_ref, mass_ref, g_ref, e_ref, noise_all, mass_all = refs[:7]
+        rest = refs[7:]
     elif kind == "crit":
         p_ref, weight_ref, readout_ref, g_ref = refs[:4]
         rest = refs[4:]
@@ -47,7 +47,8 @@
         p_ref, e_ref, g_ref = refs[:3]
         rest = refs[3:]
     (c_buf, s1_buf, x_buf, s2_buf, z_buf) = rest[:5]
-    sems = rest[5:]
+    sems = rest[5:17]
+    small_send, small_recv = rest[17:]
     cs_send, cs_recv, xs_send, xs_recv, zs_send, zs_recv = sems[:6]
     zg_send, zg_recv, xg_send, xg_recv, cg_send, cg_recv = sems[6:]
 
@@ -206,6 +207,16 @@
         for copy in started["cg", k]:
             copy.wait_recv()
 
+    small = []
+    if kind == "enc":
+        cells = noise_ref.shape[1]
+        own_cells = pl.ds(pl.multiple_of(core * cells, 16), cells)
+        small = [
+            remote(noise_ref, noise_all.at[:, own_cells, :], small_send.at[0], small_recv.at[0], other),
+            remote(mass_ref, mass_all.at[core], small_send.at[1], small_recv.at[1], other),
+        ]
+        noise_all[:, own_cells, :] = noise_ref[...]
+        mass_all[core] = mass_ref[...]
     stages = (stage0, stage1, stage2, stage3, stage4, stage5, stage6)
     for k in range(nch):
         stage0(k)
@@ -213,6 +224,9 @@
         for index in range(len(stages) - 1, 0, -1):
             if 0 <= step - index < nch:
                 stages[index](step - index)
+    for copy in small:
+        copy.wait_recv()
+    started["small"] = small
     for copies in started.values():
         for copy in copies:
             copy.wait_send()
@@ -227,8 +241,14 @@
     gathered = jax.ShapeDtypeStruct((n_rows, hidden), BF16)
     vmem = pl.BlockSpec(memory_space=pltpu.VMEM)
     if kind == "enc":
-        out_shape = (gathered, jax.ShapeDtypeStruct((n_rows // nz, quarter), F32))
-        out_specs = (vmem, vmem)
+        noise, mass = extras
+        out_shape = (
+            gathered,
+            jax.ShapeDtypeStruct((n_rows // nz, quarter), F32),
+            jax.ShapeDtypeStruct((noise.shape[0], 2 * noise.shape[1], noise.shape[2]), BF16),
+            jax.ShapeDtypeStruct((2,) + mass.shape, F32),
+        )
+        out_specs = (vmem,) * 4
     else:
         out_shape, out_specs = gathered, vmem
     dma = pltpu.SemaphoreType.DMA
@@ -245,13 +265,47 @@
             pltpu.VMEM((n_rows, quarter), BF16),
             pltpu.VMEM((nz - 1, n_rows // nz, quarter), BF16),
         ]
-        + [dma((nch, count)) for count in counts],
+        + [dma((nch, count)) for count in counts]
+        + [dma((2,)), dma((2,))],
         compiler_params=pltpu.CompilerParams(
             collective_id={"enc": 0, "crit": 1, "lat": 2}[kind],
             has_side_effects=True,
             vmem_limit_bytes=40 * 1024 * 1024,
         ),
     )(partial, *extras)
+
+
+def outer_kernel(left_ref, right_ref, out_ref):
+    width = min(1024, right_ref.shape[1])
+
+    def step(i, carry):
+        cols = pl.ds(pl.multiple_of(i * width, width), width)
+        out_ref[:, cols] = contract(left_ref[...], right_ref[:, cols], 0, 0).astype(BF16)
+        return carry
+
+    lax.fori_loop(0, right_ref.shape[1] // width, step, 0)
+
+
+def outer_sum(left, right):
+    depth, n_left = left.shape
+    n_right = right.shape[1]
+    tile = min(256, n_left)
+    return pl.pallas_call(
+        outer_kernel,
+        grid=(n_left // tile,),
+        out_shape=jax.ShapeDtypeStruct((n_left, n_right), BF16),
+        in_specs=[
+            pl.BlockSpec((depth, tile), lambda i: (0, i)),
+            pl.BlockSpec((depth, n_right), lambda i: (0, 0)),
+        ],
+        out_specs=pl.BlockSpec((tile, n_right), lambda i: (i, 0)),
+        compiler_params=pltpu.CompilerParams(vmem_limit_bytes=32 * 1024 * 1024),
+        cost_estimate=pl.CostEstimate(
+            flops=2 * depth * n_left * n_right,
+            bytes_accessed=2 * (n_left * n_right + depth * (n_left + n_right)),
+            transcendentals=0,
+        ),
+    )(left, right)
 
 
 def paired_rows(perturbed, pair_index):
@@ -271,16 +325,27 @@
     n_cells, n_genes = control_all.shape
     n_pairs = n_cells * n_draws
     hidden = w_enc.shape[1]
-    w_noise_all = lax.all_gather(w_noise, "gene", axis=1, tiled=True)
-    readout_all = lax.all_gather(readout, "gene", axis=0, tiled=True)
-    noise_all = lax.all_gather(noise_draws.transpose(1, 0, 2), "cell", axis=1, tiled=True)
-    mass_all = lax.all_gather(cell_mass, "cell", axis=0, tiled=True)
+    n_noise = w_noise.shape[0]
+    high = lax.reduce_precision(readout, 8, 7)
+    middle = lax.reduce_precision(readout - high, 8, 7)
+    terms = jnp.stack([high, middle, readout - high - middle]).astype(BF16)
+    terms = jnp.pad(terms, ((0, 13), (0, 0)))
+    packed = lax.all_gather(
+        jnp.concatenate([w_noise, terms], axis=0), "gene", axis=1, tiled=True
+    )
+    w_noise_all = packed[:n_noise]
     target = lax.all_to_all(
         paired_rows(perturbed, pair_index), "cell", split_axis=1, concat_axis=0, tiled=True
     )
 
     enc_part = contract(control_all, w_enc, 1, 0).astype(BF16)
-    silu_enc, enc_own = exchange("enc", enc_part, (), n_gene)
+    mass_rows = jnp.broadcast_to(cell_mass[None, :], (8, cell_mass.shape[0]))
+    silu_enc, enc_own, noise_all, mass_all = exchange(
+        "enc", enc_part, (noise_draws.transpose(1, 0, 2), mass_rows), n_gene
+    )
+    mass_all = mass_all[:, 0, :].reshape(n_cells)
+    read = packed[n_noise : n_noise + 3].astype(F32)
+    readout_all = read[0] + (read[1] + read[2])
     shift = contract(noise_all.reshape(n_pairs, noise_all.shape[2]), w_noise_all, 1, 0)
     latent = (
         (silu_enc.astype(F32)[None] + shift.reshape(n_draws, n_cells, hidden))
@@ -306,7 +371,7 @@
     lat_part = contract(summed, w_dec, 1, 0).astype(BF16)
     enc_grad = exchange("lat", lat_part, (enc_own,), n_gene)
     grad_dec = contract(moved_grad.reshape(n_pairs, n_genes), latent, 0, 0).astype(BF16)
-    grad_enc = contract(control_all, enc_grad, 0, 0).astype(BF16)
+    grad_enc = outer_sum(control_all, enc_grad)
     return (grad_enc, grad_dec)
 
 

time: 345 us -> 302 us (0.88)
  blocking collectives: 29.5 us -> 0 us
  local copies, waits for them, and re-layouts: 26.4 us -> 5.79 us
  Pallas kernels: 166 us -> 181 us
  matrix products: 89 us -> 77.4 us
  other arithmetic: 10.3 us -> 14 us
    all_gather x3 -> x0, blocking collectives: 29.5 us -> none  [the longest x1 21.5 us: shards(): readout_all = lax.all_gather(readout, 'gene', axis=0, tiled=True)]
    unnamed x26 -> x22, local copies, waits for them, and re-layouts: 24.1 us -> 2.38 us
    pallas_call x0 -> x1, Pallas kernels: none -> 11.9 us  [outer_sum(): pl.pallas_call(outer_kernel, grid=(n_left // tile,), out_shape=jax.ShapeD...]
    dot_general x8 -> x7, matrix products: 88.6 us -> 76.9 us  [contract(): lax.dot_general(former, latter, (((former_dim,), (latter_dim,)), ((), ())...]
  transfers between devices with their start and end apart: 3 -> 3, of which waited for: 0 -> 1; matrix products, arithmetic and copies ran while one was open for 18% -> 22% of each run, Pallas kernels for 36% -> 41%
where the time goes in v2:
time: 302 us; the launch traced here: 301 us
  Pallas kernels  181 us (60%)
  matrix products  77.4 us (26%)
  between operations  14.2 us (5%)
  other arithmetic  14 us (5%)
  starting transfers between devices  9.08 us (3%)
  local copies, waits for them, and re-layouts  5.79 us (2%)
    pallas_call x3, Pallas kernels, exchange(): pl.pallas_call(functools.partial(exchange_kernel, kind, nz, nx, nch), out...  169 us
    dot_general x7, matrix products, contract(): lax.dot_general(former, latter, (((former_dim,), (latter_dim,)), ((), ())...  76.9 us
    pallas_call x1, Pallas kernels, outer_sum(): pl.pallas_call(outer_kernel, grid=(n_left // tile,), out_shape=jax.ShapeD...  11.9 us
  transfers between devices with their start and end apart: 3, of which 1 were waited for; matrix products, arithmetic and copies ran while one was open for 22% of the time, Pallas kernels for 41%

profile of v2, /device:TPU:5, one launch (start us, length us, event | category | flops | bytes accessed | tf_op | source)
XLA Modules:
  0.0 301.2 jit_solution(5050259497081740712)
XLA Ops:
  7.2 0.0 copy-start
  7.2 0.0 copy-start.6
  7.2 0.0 copy-start.7
  7.2 0.0 all-gather.2.cloned.1.call-start
  7.2 0.8 reduce-precision_convert_fusion.1
  8.1 1.6 pad_maximum_fusion
  9.6 0.0 all-gather.2.cloned.1.call-update
  9.6 2.3 copy.35
  12.0 4.2 %all-to-all-start = ((bf16[128,2,2048]{2,0,1:T(8,128)(2,1)}), bf16[128,2,2048]{2,0,1:T(8,128)(2,1)S(1)}, u32[]{:S(2)}, u32[]{:S(2)}) async-start(bf16[128,2,2048]{2,0,1:T(8,128)(2,1)} %bitcast.52), calls=%async_computation | async-start | bytes 2097152 | tf_op jit(solution)/shard_map/all_to_all | solution.py:324
  16.2 0.0 copy-done.6
  16.2 0.0 copy-done
  16.2 0.0 copy-done.7
  16.2 0.5 convolution_convert_fusion.3
  16.7 1.1 copy.34
  17.8 0.1 all-to-all-done
  17.9 4.8 %all-to-all-start.1 = ((bf16[128,2,2048]{2,0,1:T(8,128)(2,1)}), bf16[128,2,2048]{2,0,1:T(8,128)(2,1)}, u32[]{:S(2)}, u32[]{:S(2)}) async-start(bf16[128,2,2048]{2,0,1:T(8,128)(2,1)} %bitcast.51), calls=%async_computation.1 | async-start | bytes 2097152 | tf_op jit(solution)/shard_map/all_to_all | solution.py:337
  22.7 0.0 copy-start.8
  22.8 8.4 %convolution_convert_fusion.2.refs_0_ = bf16[256,4096]{1,0:T(8,128)(2,1)S(1)} fusion(bf16[256,2048]{1,0:T(8,128)(2,1)S(1)} %bitcast.54, bf16[2048,4096]{1,0:T(8,128)(2,1)} %param.15), kind=kOutput, calls=%fused_computation.8 | convolution fusion | flops 4296015872 | bytes 19922944 | tf_op jit(solution)/shard_map/dot_general | solution.py:23
  31.2 0.0 copy-done.8
  31.2 52.3 %shard_map.113 = (bf16[256,4096]{1,0:T(8,128)(2,1)S(1)}, f32[64,1024]{1,0:T(8,128)S(1)}, bf16[2,256,128]{2,1,0:T(8,128)(2,1)S(1)}, f32[2,8,128]{2,1,0:T(8,128)S(1)}) custom-call(bf16[256,4096]{1,0:T(8,128)(2,1)S(1)} %convolution_convert_fusion.2.refs_0_, bf16[2,128,128]{2,1,0:T(8,128)(2,1)S(1)} %bitcast.57, f32[8,128]{1,0:T(8,128)S(1)} %broadcast_in_dim.2.refs_2_), custom_call_target="tpu_custom_call" | custom-call | tf_op jit(solution)/shard_map/pallas_call | solution.py:256
  83.5 0.0 copy-start.2
  83.5 1.3 copy-done.2
  84.9 0.1 copy.30
  85.0 4.1 %convert_element_type.61 = f32[256,4096]{1,0:T(8,128)} convert(bf16[256,4096]{1,0:T(8,128)(2,1)} %copy-done.2) | non-fusion elementwise | flops 1048576 | bytes 6291456 | tf_op jit(solution)/shard_map/convert_element_type | solution.py:351
  89.1 1.6 bitcast_convert_fusion.1
  90.8 0.0 all-gather.2.cloned.1.call-done
  90.8 0.8 slice_convert_fusion
  91.7 3.8 %add_convert_fusion = bf16[2,256,4096]{2,1,0:T(8,128)(2,1)S(1)} fusion(bf16[2,256,128]{2,1,0:T(8,128)(2,1)S(1)} %get-tuple-element.8, f32[256,4096]{1,0:T(8,128)} %convert_element_type.61, bf16[144,4096]{1,0:T(8,128)(2,1)} %all-gather.2.cloned.1.call-done), kind=kOutput, calls=%fused_computation.3 | convolution fusion | flops 541065216 | bytes 9568256 | tf_op jit(solution)/shard_map/dot_general | solution.py:23
  95.4 0.0 copy-start.4
  95.4 16.6 %convert_reduce_fusion = (f32[256,2048]{1,0:T(8,128)}, bf16[2,256,2048]{2,1,0:T(8,128)(2,1)}) fusion(bf16[2,256,4096]{2,1,0:T(8,128)(2,1)S(1)} %add_convert_fusion, bf16[2048,4096]{1,0:T(8,128)(2,1)} %param.16, f32[256,2048]{1,0:T(8,128)} %bitcast_convert_fusion.1), kind=kOutput, calls=%fused_computation.5 | convolution fusion | flops 8593604608 | bytes 27262976 | tf_op jit(solution)/shard_map/dot_general | solution.py:23
  112.0 0.0 copy-done.4
  112.0 13.0 %convolution_convert_fusion.refs_0_ = bf16[512,4096]{1,0:T(8,128)(2,1)S(1)} fusion(bf16[512,2048]{1,0:T(8,128)(2,1)} %bitcast.60, bf16[2048,4096]{1,0:T(8,128)(2,1)} %param.17), kind=kOutput, calls=%fused_computation.4 | convolution fusion | flops 8592031744 | bytes 23068672 | tf_op jit(solution)/shard_map/dot_general | solution.py:23
  125.0 70.3 %shard_map.114 = bf16[512,4096]{1,0:T(8,128)(2,1)S(1)} custom-call(bf16[512,4096]{1,0:T(8,128)(2,1)S(1)} %convolution_convert_fusion.refs_0_, f32[512,1]{1,0:T(8,128)S(1)} %bitcast.56, f32[1,4096]{1,0:T(1,128)S(1)} %fusion.14.refs_2_), custom_call_target="tpu_custom_call" | custom-call | tf_op jit(solution)/shard_map/pallas_call | solution.py:256
  195.3 13.8 %fusion.18 = f32[512,2048]{1,0:T(8,128)} fusion(bf16[512,4096]{1,0:T(8,128)(2,1)S(1)} %shard_map.114, bf16[2048,4096]{1,0:T(8,128)(2,1)} %param.17), kind=kOutput, calls=%fused_computation.42 | convolution fusion | flops 8589934592 | bytes 25165824 | tf_op jit(solution)/shard_map/dot_general | solution.py:23
  209.1 0.0 all-to-all-done.1
  209.1 0.0 copy-start.3
  209.1 2.3 bitcast_subtract_fusion
  211.3 0.9 copy-done.3
  212.2 2.7 fusion.16
  214.9 0.0 copy-start.5
  215.0 8.6 %convolution_convert_fusion.1.refs_0_ = bf16[256,4096]{1,0:T(8,128)(2,1)S(1)} fusion(bf16[256,2048]{1,0:T(8,128)(2,1)S(1)} %get-tuple-element.10, bf16[2048,4096]{1,0:T(8,128)(2,1)} %param.16), kind=kOutput, calls=%fused_computation.7 | convolution fusion | flops 4296015872 | bytes 19922944 | tf_op jit(solution)/shard_map/dot_general | solution.py:23
  223.5 0.0 copy-done.5
  223.5 12.8 %bitcast_convert_fusion = bf16[2048,4096]{1,0:T(8,128)(2,1)} fusion(bf16[2,256,2048]{2,1,0:T(8,128)(2,1)S(1)} %get-tuple-element.11, bf16[2,256,4096]{2,1,0:T(8,128)(2,1)S(1)} %copy-done.5), kind=kOutput, calls=%fused_computation | convolution fusion | flops 8598323200 | bytes 23068672 | tf_op jit(solution)/shard_map/dot_general | solution.py:23
  236.4 46.1 %shard_map.115.right_ref = bf16[256,4096]{1,0:T(8,128)(2,1)S(1)} custom-call(bf16[256,4096]{1,0:T(8,128)(2,1)S(1)} %convolution_convert_fusion.1.refs_0_, f32[64,1024]{1,0:T(8,128)S(1)} %get-tuple-element.9.refs_1_), custom_call_target="tpu_custom_call" | custom-call | tf_op jit(solution)/shard_map/pallas_call | solution.py:256
  282.5 0.0 copy-start.1
  282.5 11.9 %shard_map.116 = bf16[2048,4096]{1,0:T(8,128)(2,1)} custom-call(bf16[256,2048]{1,0:T(8,128)(2,1)S(1)} %bitcast.55, bf16[256,4096]{1,0:T(8,128)(2,1)S(1)} %shard_map.115.right_ref), custom_call_target="tpu_custom_call" | custom-call | flops 4294967296 | bytes 19922944 | tf_op jit(solution)/shard_map/pallas_call | solution.py:293
  294.4 0.0 copy-done.1
  (10 shorter events, 0.1 us)
Async XLA Ops:
  7.2 9.1 %copy-start = (bf16[128,4096]{1,0:T(8,128)(2,1)S(1)}, bf16[128,4096]{1,0:T(8,128)(2,1)}, u32[]{:S(2)}) copy-start(bf16[128,4096]{1,0:T(8,128)(2,1)} %param.11) | copy-start | bytes 3145732
  7.2 9.0 %copy-start.6 = (bf16[128,2,128]{2,1,0:T(2,128)(2,1)S(1)}, bf16[128,2,128]{2,1,0:T(2,128)(2,1)}, u32[]{:S(2)}) copy-start(bf16[128,2,128]{2,1,0:T(2,128)(2,1)} %param.13) | copy-start | bytes 196612
  7.2 9.0 %copy-start.7 = (s32[1,128]{1,0:T(1,128)S(1)}, s32[1,128]{1,0:T(1,128)}, u32[]{:S(2)}) copy-start(s32[1,128]{1,0:T(1,128)} %param.12) | copy-start | bytes 1540
  7.2 83.6 %all-gather.2.cloned.1.call-start = ((), (), s32[]{:S(2)}) async-start(), calls=%async_computation.2 | async-start | bytes 1327104 | tf_op jit(solution)/shard_map/all_gather | solution.py:333
  12.0 6.0 %all-to-all-start = ((bf16[128,2,2048]{2,0,1:T(8,128)(2,1)}), bf16[128,2,2048]{2,0,1:T(8,128)(2,1)S(1)}, u32[]{:S(2)}, u32[]{:S(2)}) async-start(bf16[128,2,2048]{2,0,1:T(8,128)(2,1)} %bitcast.52), calls=%async_computation | async-start | bytes 2097152 | tf_op jit(solution)/shard_map/all_to_all | solution.py:324
  17.9 191.1 %all-to-all-start.1 = ((bf16[128,2,2048]{2,0,1:T(8,128)(2,1)}), bf16[128,2,2048]{2,0,1:T(8,128)(2,1)}, u32[]{:S(2)}, u32[]{:S(2)}) async-start(bf16[128,2,2048]{2,0,1:T(8,128)(2,1)} %bitcast.51), calls=%async_computation.1 | async-start | bytes 2097152 | tf_op jit(solution)/shard_map/all_to_all | solution.py:337
  22.7 8.5 %copy-start.8 = (f32[128]{0:T(128)S(1)}, f32[128]{0:T(128)}, u32[]{:S(2)}) copy-start(f32[128]{0:T(128)} %param.14) | copy-start | bytes 1540
  83.5 1.3 copy-start.2
  95.4 16.6 %copy-start.4 = (bf16[2,256,4096]{2,1,0:T(8,128)(2,1)}, bf16[2,256,4096]{2,1,0:T(8,128)(2,1)S(1)}, u32[]{:S(2)}) copy-start(bf16[2,256,4096]{2,1,0:T(8,128)(2,1)S(1)} %add_convert_fusion) | copy-start | bytes 12582916
  209.1 3.1 %copy-start.3 = (f32[512,2048]{1,0:T(8,128)S(1)}, f32[512,2048]{1,0:T(8,128)}, u32[]{:S(2)}) copy-start(f32[512,2048]{1,0:T(8,128)} %fusion.18) | copy-start | bytes 12582916
  214.9 8.6 %copy-start.5 = (bf16[2,256,4096]{2,1,0:T(8,128)(2,1)S(1)}, bf16[2,256,4096]{2,1,0:T(8,128)(2,1)}, u32[]{:S(2)}) copy-start(bf16[2,256,4096]{2,1,0:T(8,128)(2,1)} %copy-done.4) | copy-start | bytes 12582916
  282.5 11.9 %copy-start.1 = (bf16[128,4096]{1,0:T(8,128)(2,1)S(1)}, bf16[128,4096]{1,0:T(8,128)(2,1)}, u32[]{:S(2)}) copy-start(bf16[128,4096]{1,0:T(8,128)(2,1)} %param.11) | copy-start | bytes 3145732
Sparse Core Ops, SparseCore 0:
  10.1 47.9 all-gather.1

commit v3 on v2

--- a/solution.py
+++ b/solution.py
@@ -37,22 +37,24 @@
 
 
 def exchange_kernel(kind, nz, nx, nch, *refs):
+    a_ref, w_ref = refs[:2]
+    refs = refs[2:]
     if kind == "enc":
-        p_ref, noise_ref, mass_ref, g_ref, e_ref, noise_all, mass_all = refs[:7]
-        rest = refs[7:]
+        noise_ref, mass_ref, g_ref, e_ref, noise_all, mass_all = refs[:6]
+        rest = refs[6:]
     elif kind == "crit":
-        p_ref, weight_ref, readout_ref, g_ref = refs[:4]
-        rest = refs[4:]
+        weight_ref, readout_ref, g_ref = refs[:3]
+        rest = refs[3:]
     else:
-        p_ref, e_ref, g_ref = refs[:3]
-        rest = refs[3:]
+        e_ref, g_ref = refs[:2]
+        rest = refs[2:]
     (c_buf, s1_buf, x_buf, s2_buf, z_buf) = rest[:5]
     sems = rest[5:17]
-    small_send, small_recv = rest[17:]
+    small_send, small_recv, p_ref, w_buf, w_sem = rest[17:]
     cs_send, cs_recv, xs_send, xs_recv, zs_send, zs_recv = sems[:6]
     zg_send, zg_recv, xg_send, xg_recv, cg_send, cg_recv = sems[6:]
 
-    n_rows, hidden = p_ref.shape
+    n_rows, hidden = g_ref.shape
     half = hidden // 2
     quarter = half // nx
     width = quarter // nch
@@ -78,6 +80,34 @@
 
     def z_block(which):
         return pl.ds(pl.multiple_of(which * z_rows, 16), z_rows)
+
+    order = list(range(1, nx)) + [0]
+    tiles = [(own, o, k) for k in range(nch) for own in (0, 1) for o in order]
+    slots = w_buf.shape[0]
+
+    def tile_cols(own, o, k):
+        return cols(core if own else 1 - core, (x + o) % nx, k)
+
+    def fetch(n):
+        copy = pltpu.make_async_copy(
+            w_ref.at[:, tile_cols(*tiles[n])], w_buf.at[n % slots], w_sem.at[n % slots]
+        )
+        copy.start()
+        return copy
+
+    fetched = [fetch(n) for n in range(slots)]
+
+    def multiply(*tile):
+        n = tiles.index(tile)
+        fetched[n].wait()
+        where = tile_cols(*tile)
+
+        def dot(rows, _):
+            p_ref[rows, where] = contract(a_ref[rows, :], w_buf[n % slots], 1, 0).astype(BF16)
+
+        row_loop(n_rows, min(256, n_rows), dot)
+        if n + slots < len(tiles):
+            fetched.append(fetch(n + slots))
 
     barrier = pltpu.get_barrier_semaphore()
     peers = [other] + [x_peer(o) for o in range(1, nx)] + [z_peer(o) for o in range(1, nz)]
@@ -100,16 +130,20 @@
     started = {}
 
     def stage0(k):
-        started["c", k] = [
-            remote(
-                p_ref.at[:, cols(1 - core, (x + o) % nx, k)],
-                c_buf.at[o, :, part(k)],
-                cs_send.at[k, o],
-                cs_recv.at[k, o],
-                other,
+        started["c", k] = []
+        for o in order:
+            multiply(0, o, k)
+            started["c", k].append(
+                remote(
+                    p_ref.at[:, tile_cols(0, o, k)],
+                    c_buf.at[o, :, part(k)],
+                    cs_send.at[k, o],
+                    cs_recv.at[k, o],
+                    other,
+                )
             )
-            for o in list(range(1, nx)) + [0]
-        ]
+        for o in order:
+            multiply(1, o, k)
 
     def stage1(k):
         for copy in started["c", k]:
@@ -218,9 +252,9 @@
         noise_all[:, own_cells, :] = noise_ref[...]
         mass_all[core] = mass_ref[...]
     stages = (stage0, stage1, stage2, stage3, stage4, stage5, stage6)
-    for k in range(nch):
-        stage0(k)
-    for step in range(1, nch + len(stages) - 1):
+    for step in range(nch + len(stages) - 1):
+        if step < nch:
+            stage0(step)
         for index in range(len(stages) - 1, 0, -1):
             if 0 <= step - index < nch:
                 stages[index](step - index)
@@ -232,10 +266,11 @@
             copy.wait_send()
 
 
-def exchange(kind, partial, extras, n_gene):
+def exchange(kind, former, weight, extras, n_gene):
     nx = 2 if n_gene <= 8 else 4
     nz = n_gene // nx
-    n_rows, hidden = partial.shape
+    n_rows, depth = former.shape
+    hidden = weight.shape[1]
     quarter = hidden // (2 * nx)
     nch = min(4, quarter // 128)
     gathered = jax.ShapeDtypeStruct((n_rows, hidden), BF16)
@@ -256,7 +291,7 @@
     return pl.pallas_call(
         functools.partial(exchange_kernel, kind, nz, nx, nch),
         out_shape=out_shape,
-        in_specs=[vmem] * (1 + len(extras)),
+        in_specs=[vmem, pl.BlockSpec(memory_space=pl.ANY)] + [vmem] * len(extras),
         out_specs=out_specs,
         scratch_shapes=[
             pltpu.VMEM((nx, n_rows, quarter), BF16),
@@ -266,13 +301,18 @@
             pltpu.VMEM((nz - 1, n_rows // nz, quarter), BF16),
         ]
         + [dma((nch, count)) for count in counts]
-        + [dma((2,)), dma((2,))],
+        + [dma((2,)), dma((2,))]
+        + [
+            pltpu.VMEM((n_rows, hidden), BF16),
+            pltpu.VMEM((3, depth, quarter // nch), BF16),
+            dma((3,)),
+        ],
         compiler_params=pltpu.CompilerParams(
             collective_id={"enc": 0, "crit": 1, "lat": 2}[kind],
             has_side_effects=True,
-            vmem_limit_bytes=40 * 1024 * 1024,
+            vmem_limit_bytes=50 * 1024 * 1024,
         ),
-    )(partial, *extras)
+    )(former, weight, *extras)
 
 
 def outer_kernel(left_ref, right_ref, out_ref):
@@ -338,10 +378,9 @@
         paired_rows(perturbed, pair_index), "cell", split_axis=1, concat_axis=0, tiled=True
     )
 
-    enc_part = contract(control_all, w_enc, 1, 0).astype(BF16)
     mass_rows = jnp.broadcast_to(cell_mass[None, :], (8, cell_mass.shape[0]))
     silu_enc, enc_own, noise_all, mass_all = exchange(
-        "enc", enc_part, (noise_draws.transpose(1, 0, 2), mass_rows), n_gene
+        "enc", control_all, w_enc, (noise_draws.transpose(1, 0, 2), mass_rows), n_gene
     )
     mass_all = mass_all[:, 0, :].reshape(n_cells)
     read = packed[n_noise : n_noise + 3].astype(F32)
@@ -354,9 +393,14 @@
     )
     decoded = contract(latent, w_dec, 1, 1).reshape(n_draws, n_cells, n_genes)
     moved = (control_all.astype(F32)[None] + decoded).astype(BF16)
-    crit_part = contract(moved.reshape(n_pairs, n_genes), w_crit, 1, 0).astype(BF16)
     weight = jnp.tile(8.0 / n_draws * mass_all, n_draws)[:, None]
-    critic_grad = exchange("crit", crit_part, (weight, readout_all[None, :]), n_gene)
+    critic_grad = exchange(
+        "crit",
+        moved.reshape(n_pairs, n_genes),
+        w_crit,
+        (weight, readout_all[None, :]),
+        n_gene,
+    )
     critic_back = contract(critic_grad, w_crit, 1, 1).reshape(n_draws, n_cells, n_genes)
     moved_f32 = moved.astype(F32)
     mean_moved = jnp.sum(moved_f32, axis=0) / n_draws
@@ -368,8 +412,7 @@
     )
     moved_grad = (cost_grad + critic_back).astype(BF16)
     summed = jnp.sum(moved_grad.astype(F32), axis=0).astype(BF16)
-    lat_part = contract(summed, w_dec, 1, 0).astype(BF16)
-    enc_grad = exchange("lat", lat_part, (enc_own,), n_gene)
+    enc_grad = exchange("lat", summed, w_dec, (enc_own,), n_gene)
     grad_dec = contract(moved_grad.reshape(n_pairs, n_genes), latent, 0, 0).astype(BF16)
     grad_enc = outer_sum(control_all, enc_grad)
     return (grad_enc, grad_dec)

time: 302 us -> 294 us (0.974)
  matrix products: 77.4 us -> 49.5 us
  Pallas kernels: 181 us -> 201 us
    dot_general x7 -> x4, matrix products: 76.9 us -> 49.1 us  [contract(): lax.dot_general(former, latter, (((former_dim,), (latter_dim,)), ((), ())...]
    pallas_call x3, Pallas kernels: 169 us -> 189 us  [exchange(): pl.pallas_call(functools.partial(exchange_kernel, kind, nz, nx, nch), out...]
  transfers between devices with their start and end apart: 3 -> 3, of which waited for: 1 -> 1; matrix products, arithmetic and copies ran while one was open for 22% -> 16% of each run, Pallas kernels for 41% -> 47%
where the time goes in v3:
time: 294 us; the launch traced here: 293 us
  Pallas kernels  201 us (68%)
  matrix products  49.5 us (17%)
  other arithmetic  14.4 us (5%)
  between operations  14.2 us (5%)
  starting transfers between devices  8.38 us (3%)
  local copies, waits for them, and re-layouts  5.21 us (2%)
    pallas_call x3, Pallas kernels, exchange(): pl.pallas_call(functools.partial(exchange_kernel, kind, nz, nx, nch), out...  189 us
    dot_general x4, matrix products, contract(): lax.dot_general(former, latter, (((former_dim,), (latter_dim,)), ((), ())...  49.1 us
    pallas_call x1, Pallas kernels, outer_sum(): pl.pallas_call(outer_kernel, grid=(n_left // tile,), out_shape=jax.ShapeD...  11.9 us
  transfers between devices with their start and end apart: 3, of which 1 were waited for; matrix products, arithmetic and copies ran while one was open for 16% of the time, Pallas kernels for 47%

profile of v3, /device:TPU:5, one launch (start us, length us, event | category | flops | bytes accessed | tf_op | source)
XLA Modules:
  0.0 293.2 jit_solution(13741763588087942454)
XLA Ops:
  7.2 0.0 copy-start
  7.2 0.0 copy-start.6
  7.2 0.0 copy-start.7
  7.2 0.0 all-gather.2.cloned.1.call-start
  7.2 0.8 reduce-precision_convert_fusion.1
  8.1 1.6 pad_maximum_fusion
  9.6 0.0 all-gather.2.cloned.1.call-update
  9.6 2.3 copy.35
  12.0 0.0 copy-start.8
  12.0 4.4 %all-to-all-start = ((bf16[128,2,2048]{2,0,1:T(8,128)(2,1)}), bf16[128,2,2048]{2,0,1:T(8,128)(2,1)S(1)}, u32[]{:S(2)}, u32[]{:S(2)}) async-start(bf16[128,2,2048]{2,0,1:T(8,128)(2,1)} %bitcast.46), calls=%async_computation | async-start | bytes 2097152 | tf_op jit(solution)/shard_map/all_to_all | solution.py:364
  16.3 0.0 copy-done.6
  16.4 0.0 copy-done
  16.4 0.0 copy-done.7
  16.4 0.5 convolution_convert_fusion
  16.9 1.1 copy.34
  18.0 0.1 all-to-all-done
  18.1 4.0 %all-to-all-start.1 = ((bf16[128,2,2048]{2,0,1:T(8,128)(2,1)}), bf16[128,2,2048]{2,0,1:T(8,128)(2,1)S(1)}, u32[]{:S(2)}, u32[]{:S(2)}) async-start(bf16[128,2,2048]{2,0,1:T(8,128)(2,1)} %bitcast.45), calls=%async_computation.1 | async-start | bytes 2097152 | tf_op jit(solution)/shard_map/all_to_all | solution.py:377
  22.0 0.0 copy-done.8
  22.0 57.6 %shard_map.113 = (bf16[256,4096]{1,0:T(8,128)(2,1)S(1)}, f32[64,1024]{1,0:T(8,128)S(1)}, bf16[2,256,128]{2,1,0:T(8,128)(2,1)S(1)}, f32[2,8,128]{2,1,0:T(8,128)S(1)}) custom-call(bf16[256,2048]{1,0:T(8,128)(2,1)S(1)} %bitcast.48, bf16[2048,4096]{1,0:T(8,128)(2,1)} %refs_1_.3, bf16[2,128,128]{2,1,0:T(8,128)(2,1)S(1)} %bitcast.52, ...), custom_call_target="tpu_custom_call" | custom-call | tf_op jit(solution)/shard_map/pallas_call | solution.py:291
  79.7 0.0 copy-start.4
  79.7 1.3 copy-done.4
  81.0 0.1 copy.30
  81.2 4.1 %convert_element_type.51 = f32[256,4096]{1,0:T(8,128)} convert(bf16[256,4096]{1,0:T(8,128)(2,1)} %copy-done.4) | non-fusion elementwise | flops 1048576 | bytes 6291456 | tf_op jit(solution)/shard_map/convert_element_type | solution.py:390
  85.3 1.6 bitcast_convert_fusion.1
  87.0 0.0 all-gather.2.cloned.1.call-done
  87.0 0.8 slice_convert_fusion
  87.8 5.8 %add_convert_fusion = bf16[2,256,4096]{2,1,0:T(8,128)(2,1)} fusion(bf16[2,256,128]{2,1,0:T(8,128)(2,1)S(1)} %get-tuple-element.8, f32[256,4096]{1,0:T(8,128)} %convert_element_type.51, bf16[144,4096]{1,0:T(8,128)(2,1)} %all-gather.2.cloned.1.call-done), kind=kOutput, calls=%fused_computation.3 | convolution fusion | flops 541065216 | bytes 9568256 | tf_op jit(solution)/shard_map/dot_general | solution.py:23
  93.6 15.5 %convert_reduce_fusion = (f32[256,2048]{1,0:T(8,128)}, bf16[2,256,2048]{2,1,0:T(8,128)(2,1)S(1)}) fusion(bf16[2,256,4096]{2,1,0:T(8,128)(2,1)} %add_convert_fusion, bf16[2048,4096]{1,0:T(8,128)(2,1)} %refs_1_.5, f32[256,2048]{1,0:T(8,128)} %bitcast_convert_fusion.1), kind=kOutput, calls=%fused_computation.4 | convolution fusion | flops 8593604608 | bytes 27262976 | tf_op jit(solution)/shard_map/dot_general | solution.py:23
  109.1 0.0 copy-start.2
  109.1 81.1 %shard_map.114 = bf16[512,4096]{1,0:T(8,128)(2,1)} custom-call(bf16[512,2048]{1,0:T(8,128)(2,1)S(1)} %bitcast.50, bf16[2048,4096]{1,0:T(8,128)(2,1)} %refs_1_.4, f32[512,1]{1,0:T(8,128)S(1)} %bitcast.51, f32[1,4096]{1,0:T(1,128)S(1)} %fusion.14.refs_3_), custom_call_target="tpu_custom_call" | custom-call | tf_op jit(solution)/shard_map/pallas_call | solution.py:291
  190.2 0.0 copy-done.2
  190.2 15.0 %fusion.18 = f32[512,2048]{1,0:T(8,128)} fusion(bf16[512,4096]{1,0:T(8,128)(2,1)} %shard_map.114, bf16[2048,4096]{1,0:T(8,128)(2,1)} %refs_1_.4), kind=kOutput, calls=%fused_computation.39 | convolution fusion | flops 8589934592 | bytes 25165824 | tf_op jit(solution)/shard_map/dot_general | solution.py:23
  205.2 0.0 all-to-all-done.1
  205.2 0.0 copy-start.3
  205.2 2.0 bitcast_subtract_fusion
  207.2 0.2 copy-done.3
  207.4 0.0 copy-start.5
  207.4 3.4 %fusion.16 = (bf16[256,2048]{1,0:T(8,128)(2,1)S(1)}, bf16[2,256,2048]{2,1,0:T(8,128)(2,1)S(1)}) fusion(f32[2,256,2048]{2,1,0:T(8,128)} %bitcast.53, f32[256,2048]{1,0:T(8,128)S(1)} %bitcast_subtract_fusion, bf16[2,256,2048]{2,1,0:T(8,128)(2,1)S(1)} %copy-done.3, f32[256]{0:T(256)S(1)} %bitcast.57), kind=kLoop, calls=%fused_computation.38 | loop fusion | flops 6815744 | bytes 11535360 | tf_op jit(solution)/shard_map/reduce_sum | solution.py:414
  210.9 0.0 copy-done.5
  210.9 12.8 %bitcast_convert_fusion = bf16[2048,4096]{1,0:T(8,128)(2,1)} fusion(bf16[2,256,2048]{2,1,0:T(8,128)(2,1)S(1)} %get-tuple-element.11, bf16[2,256,4096]{2,1,0:T(8,128)(2,1)S(1)} %copy-done.5), kind=kOutput, calls=%fused_computation | convolution fusion | flops 8598323200 | bytes 23068672 | tf_op jit(solution)/shard_map/dot_general | solution.py:23
  223.7 50.7 %shard_map.115.right_ref = bf16[256,4096]{1,0:T(8,128)(2,1)S(1)} custom-call(bf16[256,2048]{1,0:T(8,128)(2,1)S(1)} %get-tuple-element.10.refs_0_, bf16[2048,4096]{1,0:T(8,128)(2,1)} %refs_1_.5, f32[64,1024]{1,0:T(8,128)S(1)} %get-tuple-element.9.refs_2_), custom_call_target="tpu_custom_call" | custom-call | tf_op jit(solution)/shard_map/pallas_call | solution.py:291
  274.4 0.0 copy-start.1
  274.4 11.9 %shard_map.116 = bf16[2048,4096]{1,0:T(8,128)(2,1)} custom-call(bf16[256,2048]{1,0:T(8,128)(2,1)S(1)} %bitcast.49, bf16[256,4096]{1,0:T(8,128)(2,1)S(1)} %shard_map.115.right_ref), custom_call_target="tpu_custom_call" | custom-call | flops 4294967296 | bytes 19922944 | tf_op jit(solution)/shard_map/pallas_call | solution.py:333
  286.3 0.0 copy-done.1
  (10 shorter events, 0.1 us)
Async XLA Ops:
  7.2 9.2 %copy-start = (bf16[128,4096]{1,0:T(8,128)(2,1)S(1)}, bf16[128,4096]{1,0:T(8,128)(2,1)}, u32[]{:S(2)}) copy-start(bf16[128,4096]{1,0:T(8,128)(2,1)} %param.11) | copy-start | bytes 3145732
  7.2 9.2 %copy-start.6 = (bf16[128,2,128]{2,1,0:T(2,128)(2,1)S(1)}, bf16[128,2,128]{2,1,0:T(2,128)(2,1)}, u32[]{:S(2)}) copy-start(bf16[128,2,128]{2,1,0:T(2,128)(2,1)} %param.13) | copy-start | bytes 196612
  7.2 9.2 %copy-start.7 = (s32[1,128]{1,0:T(1,128)S(1)}, s32[1,128]{1,0:T(1,128)}, u32[]{:S(2)}) copy-start(s32[1,128]{1,0:T(1,128)} %param.12) | copy-start | bytes 1540
  7.2 79.8 %all-gather.2.cloned.1.call-start = ((), (), s32[]{:S(2)}) async-start(), calls=%async_computation.2 | async-start | bytes 1327104 | tf_op jit(solution)/shard_map/all_gather | solution.py:373
  12.0 10.1 %copy-start.8 = (f32[128]{0:T(128)S(1)}, f32[128]{0:T(128)}, u32[]{:S(2)}) copy-start(f32[128]{0:T(128)} %param.14) | copy-start | bytes 1540
  12.0 6.1 %all-to-all-start = ((bf16[128,2,2048]{2,0,1:T(8,128)(2,1)}), bf16[128,2,2048]{2,0,1:T(8,128)(2,1)S(1)}, u32[]{:S(2)}, u32[]{:S(2)}) async-start(bf16[128,2,2048]{2,0,1:T(8,128)(2,1)} %bitcast.46), calls=%async_computation | async-start | bytes 2097152 | tf_op jit(solution)/shard_map/all_to_all | solution.py:364
  18.1 187.1 %all-to-all-start.1 = ((bf16[128,2,2048]{2,0,1:T(8,128)(2,1)}), bf16[128,2,2048]{2,0,1:T(8,128)(2,1)S(1)}, u32[]{:S(2)}, u32[]{:S(2)}) async-start(bf16[128,2,2048]{2,0,1:T(8,128)(2,1)} %bitcast.45), calls=%async_computation.1 | async-start | bytes 2097152 | tf_op jit(solution)/shard_map/all_to_all | solution.py:377
  79.7 1.3 copy-start.4
  109.1 81.1 %copy-start.2 = (bf16[2,256,2048]{2,1,0:T(8,128)(2,1)}, bf16[2,256,2048]{2,1,0:T(8,128)(2,1)S(1)}, u32[]{:S(2)}) copy-start(bf16[2,256,2048]{2,1,0:T(8,128)(2,1)S(1)} %get-tuple-element.18) | copy-start | bytes 6291460
  205.2 2.2 copy-start.3
  207.4 3.4 %copy-start.5 = (bf16[2,256,4096]{2,1,0:T(8,128)(2,1)S(1)}, bf16[2,256,4096]{2,1,0:T(8,128)(2,1)}, u32[]{:S(2)}) copy-start(bf16[2,256,4096]{2,1,0:T(8,128)(2,1)} %add_convert_fusion) | copy-start | bytes 12582916
  274.4 11.9 %copy-start.1 = (bf16[128,4096]{1,0:T(8,128)(2,1)S(1)}, bf16[128,4096]{1,0:T(8,128)(2,1)}, u32[]{:S(2)}) copy-start(bf16[128,4096]{1,0:T(8,128)(2,1)} %param.11) | copy-start | bytes 3145732
Sparse Core Ops, SparseCore 0:
  10.1 46.3 all-gather.1
